TPU v7x, 32 devices: a whole 2x2x4 slice. The times are simulated.
32 devices in a mesh: row: 4 (over y, core), col: 8 (over z, x).
Axes of the slice: x: 2, y: 2, z: 4, core: 2. Of those that a mesh axis runs over, the one named last changes fastest.
Arguments:
- diag_tile: float32 [1024, 1024], P('row', 'col'), as said below
- panel_left: float32 [128, 1024, 96], P('row', 'col'), may hold values from -0.625 to 0.625
- panel_right: float32 [128, 1024, 96], P('row', 'col'), may hold values from -2.5 to 2.5
- ranks: int32 [128], replicated, may hold values from 32 to 96, as said below
- tile_rows: int32 [128], replicated, may hold values from 0 to 127, each once
Outputs:
- solved_right: float32 [128, 1024, 96], P('row', 'col')
- update_left: float32 [128, 8, 1024, 96], P('row', 'col')
Inputs may be any that keep to these rules, and one draw needn't show every extreme that they name: `ranks`: each slot's rank lies in 32 to 96; both ends occur in every draw. `tile_rows`: every tile row 0 to 127 stands in exactly one slot. diag_tile is a Matern covariance with smoothness nu = 3/2 of points in the unit square plus a positive nugget on its diagonal; it is symmetric positive definite.
All inputs are finite; a program needn't handle non-finite values.
Results may differ from a plain program's by a relative error of at most 0.0003.
Values sent between devices are 32-bit elements; how exact they have to be, the bound alone decides.
No kernel may reach another device: no remote copies, remote signals or barrier semaphores. Data moves between devices by JAX's collectives and lax.ppermute only.
A program may use at most 192 MiB of HBM per device.

v0:
```python
import jax
import jax.numpy as jnp
from jax import lax
from jax.sharding import PartitionSpec as P

TC = 1


def from_root(value, axis, source):
    kept = jnp.where(lax.axis_index(axis) == source, value, 0).astype(value.dtype)
    return lax.psum(kept, axis)


def solve_tiles(factor, tiles):
    count, width, rank_max = tiles.shape
    flat = jnp.transpose(tiles, (1, 0, 2)).reshape(width, count * rank_max)
    solved = jax.scipy.linalg.solve_triangular(factor, flat, lower=True)
    return jnp.transpose(solved.reshape(width, count, rank_max), (1, 0, 2))


def shards(diag_tile, panel_left, panel_right, ranks, tile_rows):
    highest = lax.Precision.HIGHEST
    slots, piece_rows, rank_max = panel_left.shape
    row_index = lax.axis_index("row")
    col_index = lax.axis_index("col")
    stripe = lax.all_gather(diag_tile, "row", axis=0, tiled=True)
    whole = lax.all_gather(stripe, "col", axis=1, tiled=True)
    own_ranks = lax.dynamic_slice_in_dim(ranks, row_index * slots, slots)
    own_tiles = lax.dynamic_slice_in_dim(tile_rows, row_index * slots, slots)
    keep_mask = (jnp.arange(rank_max, dtype=jnp.int32)[None, :] < own_ranks[:, None]).astype(
        jnp.float32
    )
    left_part = panel_left * keep_mask[:, None, :]
    right_part = panel_right * keep_mask[:, None, :]
    wanted = col_index * TC + jnp.arange(TC, dtype=jnp.int32)
    every_slot = jnp.arange(tile_rows.shape[0], dtype=jnp.int32)
    holder = jnp.sum(
        jnp.where(tile_rows[None, :] == wanted[:, None], every_slot[None, :], 0), axis=1
    )
    owner_row = holder // slots
    owner_slot = holder % slots
    left_full, right_full = (
        lax.all_gather(left_part, "col", axis=1, tiled=True),
        lax.all_gather(right_part, "col", axis=1, tiled=True),
    )
    factor = jnp.linalg.cholesky(whole)
    solved = solve_tiles(factor, right_full)
    candidate = lax.dynamic_index_in_dim(solved, owner_slot[0], 0, keepdims=False)
    picked = [from_root(candidate, "row", owner_row[0])]
    targets = jnp.stack(picked)
    core_block = jnp.einsum("snr,tnq->strq", solved, targets, precision=highest)
    update = jnp.einsum("snr,strq->stnq", left_full, core_block, precision=highest)
    live = (own_tiles[:, None] >= wanted[None, :]).astype(jnp.float32)
    update = update * live[:, :, None, None]
    own_rows = lax.dynamic_slice_in_dim(solved, col_index * piece_rows, piece_rows, axis=1)
    return (own_rows, update)


def solution(mesh):
    return jax.shard_map(
        shards,
        mesh=mesh,
        in_specs=(P("row", "col"), P("row", "col", None), P("row", "col", None), P(), P()),
        out_specs=(P("row", "col", None), P("row", "col", None, None)),
        check_vma=False,
    )
```

profile of v0, /device:TPU:0, one launch (start us, length us, event | category | flops | bytes accessed | tf_op | source)
XLA Modules:
  0.0 780.5 jit_solution(16596734672962263477)
XLA Ops:
  8.2 9.1 %all_gather.12 = f32[1024,128]{0,1:T(8,128)} all-gather(f32[256,128]{0,1:T(8,128)S(1)} %copy.13), channel_id=1, replica_groups=mesh['row'=4,'col'=8] {'row'}, dimensions={0}, use_global_device_ids=true | all-gather | bytes 655360 | tf_op jit(solution)/shard_map/all_gather | solution.py:26
  18.2 4.1 broadcast_multiply_fusion
  25.7 66.0 %all-gather.4.cloned.1.call-done = f32[1024,1024]{0,1:T(8,128)} async-done(((f32[1024,128]{0,1:T(8,128)}), f32[1024,1024]{0,1:T(8,128)}) %all-gather.4.cloned.1.call-update) | async-done | bytes 4194320 | tf_op jit(solution)/shard_map/all_gather | solution.py:27
  91.8 5.3 copy.14
  97.1 4.8 fusion.15
  103.9 11.7 %cholesky.223 = f32[128,128]{1,0:T(8,128)S(1)} custom-call(f32[128,128]{1,0:T(8,128)S(1)} %cholesky.580), custom_call_target="Cholesky" | custom-call | tf_op jit(solution)/shard_map/jit(cholesky)/cholesky | solution.py:46
  115.7 9.8 %custom-call.63 = f32[1,128,128]{1,2,0:T(8,128)S(1)} custom-call(f32[1,128,128]{2,1,0:T(8,128)S(1)} %get-tuple-element.78), custom_call_target="InvertDiagBlocksLowerTriangular" | custom-call | tf_op jit(solution)/shard_map/jit(cholesky)/cholesky | solution.py:46
  125.5 2.5 cholesky.255
  131.9 12.0 %cholesky.244 = f32[128,128]{1,0:T(8,128)S(1)} custom-call(f32[128,128]{1,0:T(8,128)S(1)} %cholesky.584), custom_call_target="Cholesky" | custom-call | tf_op jit(solution)/shard_map/jit(cholesky)/cholesky | solution.py:46
  144.6 9.8 %custom-call.64 = f32[1,128,128]{1,2,0:T(8,128)S(1)} custom-call(f32[1,128,128]{2,1,0:T(8,128)S(1)} %get-tuple-element.75), custom_call_target="InvertDiagBlocksLowerTriangular" | custom-call | tf_op jit(solution)/shard_map/jit(cholesky)/cholesky | solution.py:46
  157.7 11.7 %cholesky.468 = f32[128,128]{1,0:T(8,128)S(1)} custom-call(f32[128,128]{1,0:T(8,128)S(1)} %cholesky.589), custom_call_target="Cholesky" | custom-call | tf_op jit(solution)/shard_map/jit(cholesky)/cholesky | solution.py:46
  170.0 9.8 %custom-call.65 = f32[1,128,128]{1,2,0:T(8,128)S(1)} custom-call(f32[1,128,128]{2,1,0:T(8,128)S(1)} %get-tuple-element.72), custom_call_target="InvertDiagBlocksLowerTriangular" | custom-call | tf_op jit(solution)/shard_map/jit(cholesky)/cholesky | solution.py:46
  181.0 2.3 convolution_subtract_fusion.7
  183.4 11.9 %cholesky.487 = f32[128,128]{1,0:T(8,128)S(1)} custom-call(f32[128,128]{1,0:T(8,128)S(1)} %cholesky.594), custom_call_target="Cholesky" | custom-call | tf_op jit(solution)/shard_map/jit(cholesky)/cholesky | solution.py:46
  195.9 9.8 %custom-call.66 = f32[1,128,128]{1,2,0:T(8,128)S(1)} custom-call(f32[1,128,128]{2,1,0:T(8,128)S(1)} %get-tuple-element.69), custom_call_target="InvertDiagBlocksLowerTriangular" | custom-call | tf_op jit(solution)/shard_map/jit(cholesky)/cholesky | solution.py:46
  206.7 2.3 convolution_subtract_fusion.8
  209.1 11.7 %cholesky.506 = f32[128,128]{1,0:T(8,128)S(1)} custom-call(f32[128,128]{1,0:T(8,128)S(1)} %cholesky.599), custom_call_target="Cholesky" | custom-call | tf_op jit(solution)/shard_map/jit(cholesky)/cholesky | solution.py:46
  221.5 10.0 %custom-call.67 = f32[1,128,128]{1,2,0:T(8,128)S(1)} custom-call(f32[1,128,128]{2,1,0:T(8,128)S(1)} %get-tuple-element.66), custom_call_target="InvertDiagBlocksLowerTriangular" | custom-call | tf_op jit(solution)/shard_map/jit(cholesky)/cholesky | solution.py:46
  234.7 11.7 %cholesky.526 = f32[128,128]{1,0:T(8,128)S(1)} custom-call(f32[128,128]{1,0:T(8,128)S(1)} %cholesky.604), custom_call_target="Cholesky" | custom-call | tf_op jit(solution)/shard_map/jit(cholesky)/cholesky | solution.py:46
  247.1 9.8 %custom-call.68 = f32[1,128,128]{1,2,0:T(8,128)S(1)} custom-call(f32[1,128,128]{2,1,0:T(8,128)S(1)} %get-tuple-element.63), custom_call_target="InvertDiagBlocksLowerTriangular" | custom-call | tf_op jit(solution)/shard_map/jit(cholesky)/cholesky | solution.py:46
  259.9 11.7 %cholesky.546 = f32[128,128]{1,0:T(8,128)S(1)} custom-call(f32[128,128]{1,0:T(8,128)S(1)} %cholesky.609), custom_call_target="Cholesky" | custom-call | tf_op jit(solution)/shard_map/jit(cholesky)/cholesky | solution.py:46
  272.3 9.8 %custom-call.69 = f32[1,128,128]{1,2,0:T(8,128)S(1)} custom-call(f32[1,128,128]{2,1,0:T(8,128)S(1)} %get-tuple-element.60), custom_call_target="InvertDiagBlocksLowerTriangular" | custom-call | tf_op jit(solution)/shard_map/jit(cholesky)/cholesky | solution.py:46
  284.7 11.7 %cholesky.564 = f32[128,128]{1,0:T(8,128)S(1)} custom-call(f32[128,128]{1,0:T(8,128)S(1)} %convolution_subtract_fusion.11), custom_call_target="Cholesky" | custom-call | tf_op jit(solution)/shard_map/jit(cholesky)/cholesky | solution.py:46
  306.9 4.8 select_select_fusion
  311.7 23.1 %while.1 = (s32[]{:T(128)}, f32[1024,1024]{1,0:T(8,128)}, s32[8,2]{0,1:T(2,128)S(1)}, f32[8,128,128]{2,1,0:T(8,128)S(1)}, s32[]{:T(128)}) while((s32[]{:T(128)}, f32[1024,1024]{1,0:T(8,128)}, s32[8,2]{0,1:T(2,128)S(1)}, f32[8,128,128]{2,1,0:T(8,128)S(1)}, s32[]{:T(128)}) %tuple.71), condition=%wide.while_cond, body=%wide.while_body.sunk | while | flops 2 | bytes 131181 | solution.py:17
  334.8 78.8 %custom-call.70 = f32[8,128,128]{1,2,0:T(8,128)S(1)} custom-call(f32[8,128,128]{2,1,0:T(8,128)S(1)} %get-tuple-element.9), custom_call_target="InvertDiagBlocksLowerTriangular" | custom-call | tf_op jit(solution)/shard_map/jit(_solve_triangular)/triangular_solve | solution.py:17
  413.6 9.0 %fusion.75 = (f32[128,32,96]{0,2,1:T(8,128)S(1)}, f32[128,32,96]{0,2,1:T(8,128)}, f32[128,32,96]{0,2,1:T(8,128)}, f32[128,32,96]{0,2,1:T(8,128)}, f32[128,32,96]...) fusion(f32[1024,32,96]{0,2,1:T(8,128)} %bitcast.144), kind=kLoop, calls=%fused_computation.170 | loop fusion | bytes 25165824 | tf_op jit(solution)/shard_map/jit(_solve_triangular)/triangular_solve | solution.py:17
  422.6 4.5 constant_dynamic-update-slice_fusion.17
  427.1 3.5 convolution_subtract_fusion.1
  430.6 3.0 constant_dynamic-update-slice_fusion.16
  433.6 6.6 convolution_subtract_fusion.4
  440.1 3.0 constant_dynamic-update-slice_fusion.15
  443.1 9.2 %fusion.16 = f32[128,3072]{0,1:T(8,128)S(1)} fusion(f32[128,3072]{0,1:T(8,128)S(1)} %bitcast.151, f32[128,3072]{1,0:T(8,128)S(1)} %get-tuple-element.85, f32[128,3072]{1,0:T(8,128)S(1)} %get-tuple-element.84, f32[128,3072]{1,0:T(8,128)S(1)} %get-tuple-element.83, f32[1024,1024]{1,0:T(8,128)} %get-tuple-element.140), kind=kOutput, calls=%fused_computation.28 | convolution fusion | flops 1814691840 | bytes 8060928 | tf_op jit(solution)/shard_map/jit(_solve_triangular)/triangular_solve | solution.py:17
  452.3 3.5 constant_dynamic-update-slice_fusion.14
  455.8 13.1 %fusion.19 = f32[128,3072]{0,1:T(8,128)} fusion(f32[128,3072]{0,1:T(8,128)} %bitcast.152, f32[128,3072]{1,0:T(8,128)} %get-tuple-element.86, f32[128,3072]{1,0:T(8,128)} %copy-done.6, f32[128,3072]{1,0:T(8,128)S(1)} %get-tuple-element.84, f32[128,3072]{1,0:T(8,128)S(1)} %get-tuple-element.83, f32[1024,1024]{1,0:T(8,128)} %get-tuple-element.140), kind=kOutput, calls=%fused_computation.29 | convolution fusion | flops 2421030912 | bytes 9699328 | tf_op jit(solution)/shard_map/jit(_solve_triangular)/triangular_solve | solution.py:17
  468.9 4.4 constant_dynamic-update-slice_fusion.13
  473.3 14.3 %convolution_subtract_fusion.3 = f32[128,3072]{0,1:T(8,128)S(1)} fusion(f32[128,3072]{0,1:T(8,128)S(1)} %bitcast.150, f32[640,3072]{1,0:T(8,128)S(1)} %get-tuple-element.40, f32[1024,1024]{1,0:T(8,128)} %get-tuple-element.140), kind=kOutput, calls=%fused_computation.26 | convolution fusion | flops 3020292096 | bytes 11337728 | tf_op jit(solution)/shard_map/jit(_solve_triangular)/triangular_solve | solution.py:17
  487.5 2.8 constant_dynamic-update-slice_fusion.12
  490.3 17.0 %convolution_subtract_fusion = f32[128,3072]{0,1:T(8,128)S(1)} fusion(f32[128,3072]{0,1:T(8,128)S(1)} %bitcast.146, f32[768,3072]{1,0:T(8,128)S(1)} %get-tuple-element.36, f32[1024,1024]{1,0:T(8,128)} %get-tuple-element.140), kind=kOutput, calls=%fused_computation.23 | convolution fusion | flops 3624271872 | bytes 12976128 | tf_op jit(solution)/shard_map/jit(_solve_triangular)/triangular_solve | solution.py:17
  507.3 2.7 constant_dynamic-update-slice_fusion.11
  510.0 20.1 %convolution_subtract_fusion.2 = f32[128,3072]{0,1:T(8,128)S(1)} fusion(f32[128,3072]{0,1:T(8,128)S(1)} %bitcast.145, f32[896,3072]{1,0:T(8,128)S(1)} %get-tuple-element.32, f32[1024,1024]{1,0:T(8,128)} %get-tuple-element.140), kind=kOutput, calls=%fused_computation.25 | convolution fusion | flops 4228251648 | bytes 14614528 | tf_op jit(solution)/shard_map/jit(_solve_triangular)/triangular_solve | solution.py:17
  530.1 2.7 convolution_dynamic-update-slice_fusion
  532.8 12.7 %copy.15 = f32[1024,3072]{0,1:T(8,128)} copy(f32[1024,3072]{1,0:T(8,128)} %convolution_dynamic-update-slice_fusion) | data formatting | bytes 25165824 | tf_op jit(solution)/shard_map/jit(_solve_triangular)/triangular_solve | solution.py:17
  547.9 2.7 dynamic-slice_bitcast_fusion
  550.5 27.4 %all-reduce.3.cloned.1.call-done = f32[1024,96]{0,1:T(8,128)} async-done(((f32[1024,96]{0,1:T(8,128)}), f32[1024,96]{0,1:T(8,128)}) %all-reduce.3.cloned.1.call-update) | async-done | bytes 393232 | tf_op jit(solution)/shard_map/psum | solution.py:11
  578.0 17.1 %fusion.38 = f32[96,32,96]{2,0,1:T(8,128)S(1)} fusion(f32[32,1024,96]{1,2,0:T(8,128)} %bitcast.143, f32[1024,96]{0,1:T(8,128)} %all-reduce.3.cloned.1.call-done), kind=kOutput, calls=%fused_computation.62 | convolution fusion | flops 3623878656 | bytes 14155776 | tf_op jit(solution)/shard_map/snr,tnq->strq/dot_general | solution.py:51
  595.0 161.6 %all-gather.8.cloned.1.call-done = f32[32,1024,96]{1,2,0:T(8,128)} async-done(((f32[32,128,96]{1,2,0:T(8,128)}), f32[32,1024,96]{1,2,0:T(8,128)}) %all-gather.8.cloned.1.call-update) | async-done | bytes 12582928 | tf_op jit(solution)/shard_map/all_gather | solution.py:43
  756.7 16.9 %fusion = f32[32,1,1024,96]{2,3,1,0:T(8,128)} fusion(f32[32]{0:T(128)S(1)} %compare_convert_fusion, f32[32,1024,96]{1,2,0:T(8,128)} %all-gather.8.cloned.1.call-done, f32[96,32,96]{2,0,1:T(8,128)S(1)} %fusion.38), kind=kOutput, calls=%fused_computation.3 | convolution fusion | flops 3627024384 | bytes 26345600 | tf_op jit(solution)/shard_map/snr,strq->stnq/dot_general | solution.py:52
  (92 shorter events, 57.7 us)
Async XLA Ops:
  7.2 84.6 %all-gather.4.cloned.1.call-start = ((), (), s32[]{:S(2)}) async-start(), calls=%async_computation | async-start | bytes 4718592 | tf_op jit(solution)/shard_map/all_gather | solution.py:27
  17.3 5.1 copy-start.7
  17.4 396.3 %all-gather.6.cloned.1.call-start = ((), (), s32[]{:S(2)}) async-start(), calls=%async_computation.1 | async-start | bytes 14155776 | tf_op jit(solution)/shard_map/all_gather | solution.py:44
  22.4 555.6 %all-reduce.3.cloned.1.call-start = ((), (), s32[]{:S(2)}) async-start(), calls=%async_computation.2 | async-start | bytes 786432 | tf_op jit(solution)/shard_map/psum | solution.py:11
  102.0 2.0 copy-start
  422.6 4.5 copy-start.3
  430.6 3.0 copy-start.2
  440.1 3.0 copy-start.5
  443.1 12.7 %copy-start.6 = (f32[128,3072]{1,0:T(8,128)}, f32[128,3072]{1,0:T(8,128)S(1)}, u32[]{:S(2)}) copy-start(f32[128,3072]{1,0:T(8,128)S(1)} %get-tuple-element.85) | copy-start | bytes 4718596
  468.9 4.4 copy-start.4
  487.5 2.8 copy-start.1
  547.2 209.4 %all-gather.8.cloned.1.call-start = ((), (), s32[]{:S(2)}) async-start(), calls=%async_computation.3 | async-start | bytes 14155776 | tf_op jit(solution)/shard_map/all_gather | solution.py:43
Sparse Core Ops, SparseCore 0:
  17.5 74.2 all-gather.3
  94.4 176.0 all-gather.5
  547.3 30.5 all-reduce.2
  580.1 176.5 all-gather.7
where the time goes:
time: 791 us; the launch traced here: 781 us
  other arithmetic  268 us (34%)
  waiting for transfers between devices  256 us (32%)
  matrix products  167 us (21%)
  local copies, waits for them, and re-layouts  58.9 us (7%)
  between operations  22 us (3%)
  blocking collectives  9.11 us (1%)
    another operation x30, other arithmetic, shards(): factor = jnp.linalg.cholesky(whole)  172 us
    all_gather x1, waiting for transfers between devices, shards(): lax.all_gather(left_part, 'col', axis=1, tiled=True)  162 us
    another operation x15, matrix products, solve_tiles(): solved = jax.scipy.linalg.solve_triangular(factor, flat, lower=True)  110 us
    another operation x3, other arithmetic, solve_tiles(): solved = jax.scipy.linalg.solve_triangular(factor, flat, lower=True)  83.6 us
    all_gather x1, waiting for transfers between devices, shards(): whole = lax.all_gather(stripe, 'col', axis=1, tiled=True)  66 us
    psum x1, waiting for transfers between devices, from_root(): return lax.psum(kept, axis)  27.4 us
    another operation x24, local copies, waits for them, and re-layouts  22.9 us
    another operation x14, matrix products, shards(): factor = jnp.linalg.cholesky(whole)  22.9 us
  transfers between devices with their start and end apart: 4, of which 3 were waited for; matrix products, arithmetic and copies ran while one was open for 44% of the time, Pallas kernels for 0%

commit v1 on v0

v1 whole, which is shorter than its diff:
```python
import functools
import jax
import jax.numpy as jnp
from jax import lax
from jax.experimental import pallas as pl
from jax.experimental.pallas import tpu as pltpu
from jax.sharding import PartitionSpec as P

F32 = jnp.float32
BF16 = jnp.bfloat16
HIGHEST = lax.Precision.HIGHEST
B = 128
MIB = 2**20


def sub_row(v, k):
    return jnp.broadcast_to(v[k : k + 1, :], v.shape)


def lane_col(v, c):
    return jnp.broadcast_to(v[:, c : c + 1], v.shape)


def inverse_factor(rows):
    lane = lax.broadcasted_iota(jnp.int32, (8, B), 1)
    sub = lax.broadcasted_iota(jnp.int32, (8, B), 0)
    work, out = list(rows), []
    for p in range(len(rows)):
        base = 8 * p
        cols = {q: [lane_col(work[q], base + j) for j in range(8)] for q in range(p, len(rows))}
        t = list(cols[p])
        in_panel = (lane >= base) & (lane < base + 8)
        r = jnp.where(in_panel, jnp.where(lane - base == sub, 1.0, 0.0).astype(F32), work[p])
        g = jnp.zeros((8, B), F32)
        for k in range(0, 8, 2):
            a, b, c = sub_row(t[k], k), sub_row(t[k], k + 1), sub_row(t[k + 1], k + 1)
            det = a * c - b * b
            inv = 1.0 / det
            pivot = (sub == k) | (sub == k + 1)
            t0 = jnp.where(pivot, jnp.where(sub == k, -1.0, 0.0).astype(F32), t[k])
            t1 = jnp.where(pivot, jnp.where(sub == k, 0.0, -1.0).astype(F32), t[k + 1])
            alpha = (t0 * c - t1 * b) * inv
            beta = (t1 * a - t0 * b) * inv
            x, y = sub_row(r, k), sub_row(r, k + 1)
            g0 = x * lax.rsqrt(a)
            g1 = (a * y - b * x) * lax.rsqrt(a * det)
            g = jnp.where(sub == k, g0, jnp.where(sub == k + 1, g1, g))
            r = jnp.where(pivot, 0.0, r) - alpha * x - beta * y
            for j in range(k + 2, 8):
                t[j] = jnp.where(pivot, 0.0, t[j]) - alpha * sub_row(t[j], k) - beta * sub_row(t[j], k + 1)
        out.append(jnp.where(lane <= sub + base, g, 0.0))
        z = [sub_row(r, j) for j in range(8)]
        for q in range(p + 1, len(rows)):
            acc = jnp.where(in_panel, 0.0, work[q])
            for j in range(8):
                acc = acc - cols[q][j] * z[j]
            work[q] = acc
    return out


def eliminate(w, g, y, k0, k1, blocks):
    for k in range(k0, k1):
        lo = B * k
        rows = [w[lo + 8 * q : lo + 8 * q + 8, lo : lo + B] for q in range(B // 8)]
        for q, piece in enumerate(inverse_factor(rows)):
            g[8 * q : 8 * q + 8, :] = piece
        y[...] = jnp.dot(g[...], w[lo : lo + B, :], precision=HIGHEST, preferred_element_type=F32)
        y[:, lo : lo + B] = g[...]
        w[lo : lo + B, :] = y[...]

        def body(i, carry):
            at = pl.multiple_of(i * B, B)
            w[pl.ds(at, B), lo : lo + B] = jnp.zeros((B, B), F32)
            w[pl.ds(at, B), :] -= lax.dot_general(
                y[:, pl.ds(at, B)], y[...], (((0,), (0,)), ((), ())), precision=HIGHEST, preferred_element_type=F32
            )
            return carry

        if k + 1 < blocks:
            lax.fori_loop(k + 1, blocks, body, 0)


def first_kernel(k1, blocks, masks, place, near, far, w, g, y):
    height, width = near.shape[1:]
    me_row, me_col = place[0], place[1]
    core = me_row % 2
    for m, (even, odd) in enumerate(masks):
        for flip, buf in ((0, near), (1, far)):
            odd_core = (core + flip) % 2
            row = (me_row ^ flip) ^ jnp.where(odd_core == 0, even[0], odd[0])
            col = me_col ^ jnp.where(odd_core == 0, even[1], odd[1])
            w[pl.ds(pl.multiple_of(row * height, 8), height), pl.ds(pl.multiple_of(col * width, B), width)] = buf[m]
    eliminate(w, g, y, 0, k1, blocks)


def whole_kernel(k1, blocks, w_in, w, g, y):
    w[...] = w_in[...]
    eliminate(w, g, y, 0, k1, blocks)


def next_kernel(k0, k1, blocks, w_in, w, g, y):
    w[...] = w_in[...]
    eliminate(w, g, y, k0, k1, blocks)


VM = pl.BlockSpec(memory_space=pltpu.VMEM)
SM = pl.BlockSpec(memory_space=pltpu.SMEM)


def elimination_call(kernel, order, specs, args):
    return pl.pallas_call(
        kernel,
        out_shape=jax.ShapeDtypeStruct((order, order), F32),
        in_specs=specs,
        out_specs=VM,
        scratch_shapes=[pltpu.VMEM((B, B), F32), pltpu.VMEM((B, order), F32)],
        compiler_params=pltpu.CompilerParams(vmem_limit_bytes=20 * MIB),
        cost_estimate=pl.CostEstimate(flops=4 * 10**9, bytes_accessed=8 * MIB, transcendentals=0),
    )(*args)


def split(v):
    high = v.astype(BF16)
    return high, (v - high.astype(F32)).astype(BF16)


def dot_tt(a, b):
    return lax.dot_general(a, b, (((1,), (1,)), ((), ())), preferred_element_type=F32)


def solve_kernel(masks, joined, n_own, n_all, width_cols, rank_max, *refs):
    if joined:
        inv, own, tgt, solved, core, xh, xl, ih, il, sh, sl = refs
    else:
        place, inv, own, near, far, solved, core, xh, xl, ih, il, sh, sl = refs
    blocks = inv.shape[0] // B
    for i in range(blocks):
        rows = slice(B * i, B * i + B)
        wide = B * (i + 1)
        ih[rows, :wide], il[rows, :wide] = split(inv[rows, :wide])
        if i % 2 == 0:
            ih[rows, wide : wide + B] = jnp.zeros((B, B), BF16)
            il[rows, wide : wide + B] = jnp.zeros((B, B), BF16)
    for c in range(blocks):
        xh[:n_own, B * c : B * c + B], xl[:n_own, B * c : B * c + B] = split(own[c])
        if joined:
            xh[n_own:, B * c : B * c + B], xl[n_own:, B * c : B * c + B] = split(tgt[c])
    if not joined:
        height, width = near.shape[1:]
        me_row, me_col = place[0], place[1]
        core_bit = me_row % 2
        for m, (even, odd) in enumerate(masks):
            for flip, buf in ((0, near), (1, far)):
                odd_core = (core_bit + flip) % 2
                row = (me_row ^ flip) ^ jnp.where(odd_core == 0, even[0], odd[0])
                col = me_col ^ jnp.where(odd_core == 0, even[1], odd[1])
                part = place[2 + row]
                high, low = split(buf[m])
                at = (pl.ds(pl.multiple_of(n_own + part * height, 16), height), pl.ds(pl.multiple_of(col * width, B), width))
                xh[at] = high
                xl[at] = low
    chunk = n_own

    def body(t, carry):
        at = pl.ds(pl.multiple_of(t * chunk, 16), chunk)
        for i in range(blocks // 2):
            deep = 2 * B * (i + 1)
            out = slice(2 * B * i, deep)
            h, l = xh[at, :deep], xl[at, :deep]
            gh, gl = ih[out, :deep], il[out, :deep]
            res = dot_tt(h, gh) + dot_tt(h, gl) + dot_tt(l, gh)
            sh[at, out], sl[at, out] = split(res)

            @pl.when(t == 0)
            def _():
                solved[2 * i] = res[:, :B]
                solved[2 * i + 1] = res[:, B:]

        return carry

    lax.fori_loop(0, n_all // chunk, body, 0)
    oh, ol = sh.at[:n_own], sl.at[:n_own]

    def core_body(j, carry):
        at = pl.ds(pl.multiple_of(n_own + j * rank_max, 16), rank_max)
        h, l = sh[at, :], sl[at, :]
        core[j] = dot_tt(h, oh[...]) + dot_tt(h, ol[...]) + dot_tt(l, oh[...])
        return carry

    lax.fori_loop(0, width_cols, core_body, 0)


def update_kernel(n, group, offs, ranks, tiles, col, core, *refs):
    own, fw, bw, out, us = refs[0], refs[1 : n], refs[n : 2 * n - 1], refs[2 * n - 1], refs[2 * n]
    step = pl.program_id(0)
    count = pl.num_programs(0)
    rank_max = own.shape[1]
    width = own.shape[2]
    row_id = lax.broadcasted_iota(jnp.int32, (rank_max, rank_max), 1)
    for s in range(group):
        def place(at, v):
            high, low = split(v)
            us[:rank_max, at] = high
            us[rank_max:, at] = low

        def spot(i):
            return pl.ds(pl.multiple_of(offs[i], width), width)

        place(spot(0), own[s])

        @pl.when(step < count // 2)
        def _():
            for k in range(n - 1):
                place(spot(1 + k), fw[k][s])

        @pl.when(step >= count // 2)
        def _():
            for k in range(n - 1):
                place(spot(n + k), bw[k][s])

        slot = step * group + s
        keep = (row_id < ranks[slot]) & (tiles[slot] >= col[0])
        c = jnp.where(keep, core[0, :, rank_max * s : rank_max * s + rank_max], 0.0)
        ch, cl = split(c)
        u = us[...]
        lhs = jnp.concatenate([ch, ch], axis=1)
        res = jnp.dot(lhs, u, preferred_element_type=F32)
        res = res + jnp.dot(cl, u[:rank_max], preferred_element_type=F32)
        out[s, 0] = res


def pick_kernel(slots, mine, ranks, right, out):
    j = pl.program_id(0)
    rank_max = right.shape[1]
    rows = lax.broadcasted_iota(jnp.int32, right.shape[1:], 0)
    keep = rows < jnp.where(mine[j] == 1, ranks[j], 0)
    out[0] = jnp.where(keep, right[0], 0.0)


def phases(rows, cols):
    even = []
    bit = cols // 2
    while bit > 1:
        even.append((0, bit))
        bit //= 2
    bit = rows // 2
    while bit > 2:
        even.append((bit, 0))
        bit //= 2
    odd = even + [(2, 0), (0, 1)]
    even = even + [(0, 1), (2, 0)]
    return even, odd


def gather_masks(rows, cols):
    even, odd = phases(rows, cols)

    def masks(steps):
        got = [(0, 0)]
        for r, c in steps:
            got = got + [(a ^ r, b ^ c) for a, b in got]
        return got

    return list(zip(masks(even), masks(odd)))


def gather_halves(piece, rows, cols):
    even, odd = phases(rows, cols)
    buf = piece[None]
    for e, o in zip(even, odd):
        pairs = []
        for r in range(rows):
            dr, dc = o if r % 2 else e
            for c in range(cols):
                pairs.append((r * cols + c, (r ^ dr) * cols + (c ^ dc)))
        buf = jnp.concatenate([buf, lax.ppermute(buf, ("row", "col"), pairs)], axis=0)
    swap = [(r, r ^ 1) for r in range(rows)]
    return buf, lax.ppermute(buf, "row", swap)


def ring_order(n):
    return list(range(0, n, 2)) + list(range(n - 1, 0, -2))


def shards(rows, cols, diag_tile, panel_left, panel_right, ranks, tile_rows):
    slots, piece_rows, rank_max = panel_left.shape
    order = piece_rows * cols
    blocks = order // B
    group = slots // cols
    row_index = lax.axis_index("row")
    col_index = lax.axis_index("col")
    masks = gather_masks(rows, cols)
    fits = piece_rows % B == 0 and blocks == cols
    left = jnp.transpose(panel_left, (0, 2, 1))
    right = jnp.transpose(panel_right, (0, 2, 1))
    own_ranks = lax.dynamic_slice_in_dim(ranks, row_index * slots, slots)
    own_tiles = lax.dynamic_slice_in_dim(tile_rows, row_index * slots, slots)

    def source_flat():
        even = jnp.array([e for e, _ in masks], jnp.int32)
        odd = jnp.array([o for _, o in masks], jnp.int32)
        is_odd = row_index % 2
        near = jnp.where(is_odd == 0, even, odd)
        far = jnp.where(is_odd == 0, odd, even)
        r = jnp.concatenate([row_index ^ near[:, 0], row_index ^ 1 ^ far[:, 0]])
        c = jnp.concatenate([col_index ^ near[:, 1], col_index ^ far[:, 1]])
        return r, c

    near, far = gather_halves(diag_tile, rows, cols)

    keep = jnp.arange(rank_max, dtype=jnp.int32)[None, :] < own_ranks[:, None]
    right_part = jnp.where(keep[:, :, None], right, 0.0)
    own = lax.all_to_all(right_part.reshape(cols, group, rank_max, piece_rows), "col", split_axis=0, concat_axis=0, tiled=True)
    own = own.reshape(cols, group * rank_max, piece_rows)

    wanted = jnp.arange(cols, dtype=jnp.int32)
    every_slot = jnp.arange(tile_rows.shape[0], dtype=jnp.int32)
    holder = jnp.sum(jnp.where(tile_rows[None, :] == wanted[:, None], every_slot[None, :], 0), axis=1)
    mine = (holder // slots == row_index).astype(jnp.int32)
    target_ranks = jnp.sum(jnp.where(tile_rows[None, :] == wanted[:, None], ranks[None, :], 0), axis=1)
    part = pl.pallas_call(
        pick_kernel,
        out_shape=jax.ShapeDtypeStruct((cols, rank_max, piece_rows), F32),
        grid_spec=pltpu.PrefetchScalarGridSpec(
            num_scalar_prefetch=3,
            grid=(cols,),
            in_specs=[pl.BlockSpec((1, rank_max, piece_rows), lambda j, s, m, r: (s[j], 0, 0))],
            out_specs=pl.BlockSpec((1, rank_max, piece_rows), lambda j, s, m, r: (j, 0, 0)),
        ),
    )(holder % slots, mine, target_ranks, right)
    bit = 1
    while bit < rows:
        half = part.shape[0] // 2
        side = (row_index // bit) % 2
        kept = lax.dynamic_slice_in_dim(part, side * half, half, 0)
        sent = lax.dynamic_slice_in_dim(part, (1 - side) * half, half, 0)
        part = kept + lax.ppermute(sent, "row", [(r, r ^ bit) for r in range(rows)])
        bit *= 2
    per = part.shape[0]
    places = []
    for r in range(rows):
        at, half, b = 0, rows // 2, 1
        while b < rows:
            at += half * ((r // b) % 2)
            half //= 2
            b *= 2
        places.append(at)
    t_near, t_far = gather_halves(part.reshape(per * rank_max, piece_rows), rows, cols)

    cycle = ring_order(cols)
    forward = [(cycle[i], cycle[(i + 1) % cols]) for i in range(cols)]
    backward = [(b, a) for a, b in forward]
    half = slots // 2
    fw, bw = [], []
    a, b = left[:half], left[half:]
    for _ in range(cols - 1):
        a = lax.ppermute(a, "col", forward)
        b = lax.ppermute(b, "col", backward)
        fw.append(a)
        bw.append(b)

    place = jnp.concatenate([jnp.stack([row_index, col_index]).astype(jnp.int32), jnp.array(places, jnp.int32)])
    per_call = 2
    if fits:
        inv = elimination_call(
            functools.partial(first_kernel, per_call, blocks, masks), order, [SM, VM, VM], (place, near, far)
        )
    else:
        r, c = source_flat()
        pieces = jnp.concatenate([near, far], axis=0)
        tile = jnp.zeros((rows * cols,) + pieces.shape[1:], F32).at[r * cols + c].set(pieces)
        tile = tile.reshape(rows, cols, order // rows, piece_rows).transpose(0, 2, 1, 3).reshape(order, order)
        inv = elimination_call(functools.partial(whole_kernel, per_call, blocks), order, [VM], (tile,))
    for k in range(per_call, blocks, per_call):
        inv = elimination_call(functools.partial(next_kernel, k, k + per_call, blocks), order, [VM], (inv,))

    n_own, n_tgt = group * rank_max, cols * rank_max
    n_all = n_own + n_tgt
    if fits:
        extra, specs = (t_near, t_far), [SM, VM, VM, VM, VM]
        args = (place, inv, own) + extra
    else:
        own = own.transpose(1, 0, 2).reshape(n_own, blocks, B).transpose(1, 0, 2)
        r, c = source_flat()
        spots = jnp.array(places, jnp.int32)[r]
        pieces = jnp.concatenate([t_near, t_far], axis=0)
        tgt = jnp.zeros((rows * cols,) + pieces.shape[1:], F32).at[spots * cols + c].set(pieces)
        tgt = tgt.reshape(rows, cols, per * rank_max, piece_rows).transpose(0, 2, 1, 3).reshape(n_tgt, blocks, B)
        args, specs = (inv, own, tgt.transpose(1, 0, 2)), [VM, VM, VM]
    solved, core = pl.pallas_call(
        functools.partial(solve_kernel, masks, not fits, n_own, n_all, cols, rank_max),
        out_shape=[
            jax.ShapeDtypeStruct((blocks, n_own, B), F32),
            jax.ShapeDtypeStruct((cols, rank_max, n_own), F32),
        ],
        in_specs=specs,
        out_specs=[VM, VM],
        scratch_shapes=[
            pltpu.VMEM((n_all, order), BF16),
            pltpu.VMEM((n_all, order), BF16),
            pltpu.VMEM((order, order), BF16),
            pltpu.VMEM((order, order), BF16),
            pltpu.VMEM((n_all, order), BF16),
            pltpu.VMEM((n_all, order), BF16),
        ],
        compiler_params=pltpu.CompilerParams(vmem_limit_bytes=50 * MIB),
        cost_estimate=pl.CostEstimate(flops=6 * 10**9, bytes_accessed=12 * MIB, transcendentals=0),
    )(*args)
    core = lax.all_to_all(core, "col", split_axis=0, concat_axis=0, tiled=True)
    if not fits:
        solved = solved.transpose(1, 0, 2).reshape(n_own, cols, piece_rows).transpose(1, 0, 2)
    back = lax.all_to_all(solved, "col", split_axis=0, concat_axis=0, tiled=True)
    own_rows = back.reshape(slots, rank_max, piece_rows)

    at = jnp.array([cycle.index(c) for c in range(cols)], jnp.int32)[col_index]
    cyc = jnp.array(cycle, jnp.int32)
    ks = jnp.arange(1, cols, dtype=jnp.int32)
    offs = jnp.concatenate([col_index[None], cyc[(at - ks) % cols], cyc[(at + ks) % cols]]).astype(jnp.int32) * piece_rows
    if fits:
        last = cols // 2 - 1
        u_spec = pl.BlockSpec((group, rank_max, piece_rows), lambda c, *_: (c, 0, 0))
        f_spec = pl.BlockSpec((group, rank_max, piece_rows), lambda c, *_: (jnp.minimum(c, last), 0, 0))
        b_spec = pl.BlockSpec((group, rank_max, piece_rows), lambda c, *_: (jnp.maximum(c - last - 1, 0), 0, 0))
        update = pl.pallas_call(
            functools.partial(update_kernel, cols, group),
            out_shape=jax.ShapeDtypeStruct((slots, 1, rank_max, order), F32),
            grid_spec=pltpu.PrefetchScalarGridSpec(
                num_scalar_prefetch=4,
                grid=(cols,),
                in_specs=[pl.BlockSpec((1, rank_max, n_own), lambda c, *_: (c, 0, 0)), u_spec]
                + [f_spec] * (cols - 1)
                + [b_spec] * (cols - 1),
                out_specs=pl.BlockSpec((group, 1, rank_max, order), lambda c, *_: (c, 0, 0, 0)),
                scratch_shapes=[pltpu.VMEM((2 * rank_max, order), BF16)],
            ),
            compiler_params=pltpu.CompilerParams(vmem_limit_bytes=40 * MIB),
        )(offs, own_ranks, own_tiles, col_index[None].astype(jnp.int32), core, left, *fw, *bw)
        update = jnp.transpose(update, (0, 1, 3, 2))
    else:
        spots = offs // piece_rows
        halves = []
        for h, ring in enumerate((fw, bw)):
            pieces = jnp.stack([left[h * half : h * half + half]] + ring)
            where = jnp.concatenate([spots[:1], spots[1 + h * (cols - 1) : 1 + (h + 1) * (cols - 1)]])
            halves.append(jnp.zeros_like(pieces).at[where].set(pieces))
        full = jnp.concatenate(halves, axis=1).transpose(1, 2, 0, 3).reshape(slots, rank_max, order)
        core = core.reshape(cols, rank_max, group, rank_max).transpose(0, 2, 3, 1).reshape(slots, rank_max, rank_max)
        live = (own_tiles >= col_index)[:, None, None] & keep[:, :, None]
        core = jnp.where(live, core, 0.0)
        update = jnp.einsum("srn,srq->snq", full, core, precision=HIGHEST)[:, None]
    return (jnp.transpose(own_rows, (0, 2, 1)), update)


def solution(mesh):
    return jax.shard_map(
        functools.partial(shards, mesh.shape["row"], mesh.shape["col"]),
        mesh=mesh,
        in_specs=(P("row", "col"), P("row", "col", None), P("row", "col", None), P(), P()),
        out_specs=(P("row", "col", None), P("row", "col", None, None)),
        check_vma=False,
    )
```

time: 791 us -> 397 us (0.50)
  other arithmetic: 268 us -> 10.3 us
  matrix products: 167 us -> 0 us
  Pallas kernels: 0 us -> 103 us
  waiting for transfers between devices: 256 us -> 162 us
  starting transfers between devices: 0.16 us -> 83.5 us
  local copies, waits for them, and re-layouts: 58.9 us -> 31.1 us
  between operations: 22 us -> 1.25 us
  blocking collectives: 9.11 us -> 0 us
    another operation x33 -> x0, other arithmetic: 256 us -> none  [the longest x30 172 us: shards(): factor = jnp.linalg.cholesky(whole)]
    all_gather x3 -> x0, waiting for transfers between devices: 228 us -> none  [the longest x1 162 us: shards(): lax.all_gather(left_part, 'col', axis=1, tiled=True)]
    ppermute x0 -> x26, waiting for transfers between devices: none -> 162 us  [the longest x7 118 us: shards(): b = lax.ppermute(b, 'col', backward)]
    another operation x29 -> x0, matrix products: 133 us -> none  [the longest x15 110 us: solve_tiles(): solved = jax.scipy.linalg.solve_triangular(factor, flat, lower=True)]
    pallas_call x0 -> x7, Pallas kernels: none -> 103 us  [the longest x4 58.2 us: elimination_call(): pl.pallas_call(kernel, out_shape=jax.ShapeDtypeStruct((order, order), F32...]
    ppermute x0 -> x26, starting transfers between devices: none -> 67.2 us  [the longest x7 21 us: shards(): a = lax.ppermute(a, 'col', forward)]
    another operation x35 -> x0, local copies, waits for them, and re-layouts: 47.2 us -> none
    dot_general x2 -> x0, matrix products: 34 us -> none  [the longest x1 17.1 us: shards(): core_block = jnp.einsum('snr,tnq->strq', solved, targets, precision=highest)]
  transfers between devices with their start and end apart: 4 -> 29, of which waited for: 3 -> 16; matrix products, arithmetic and copies ran while one was open for 44% -> 6% of each run, Pallas kernels for 0% -> 26%
where the time goes in v1:
time: 397 us; the launch traced here: 391 us
  waiting for transfers between devices  162 us (41%)
  Pallas kernels  103 us (26%)
  starting transfers between devices  83.5 us (21%)
  local copies, waits for them, and re-layouts  31.1 us (8%)
  other arithmetic  10.3 us (3%)
    ppermute x7, waiting for transfers between devices, shards(): b = lax.ppermute(b, 'col', backward)  118 us
    pallas_call x4, Pallas kernels, elimination_call(): pl.pallas_call(kernel, out_shape=jax.ShapeDtypeStruct((order, order), F32...  58.2 us
    ppermute x8, waiting for transfers between devices, gather_halves(): lax.ppermute(buf, ('row', 'col'), pairs)  23.1 us
    pallas_call x1, Pallas kernels, shards(): pl.pallas_call(functools.partial(solve_kernel, masks, not fits, n_own, n_...  22.6 us
    ppermute x7, starting transfers between devices, shards(): a = lax.ppermute(a, 'col', forward)  21 us
    unnamed x47, local copies, waits for them, and re-layouts  20.6 us
    ppermute x2, starting transfers between devices, gather_halves(): return (buf, lax.ppermute(buf, 'row', swap))  19.8 us
    pallas_call x1, Pallas kernels, shards(): pl.pallas_call(functools.partial(update_kernel, cols, group), out_shape=j...  16.6 us
  transfers between devices with their start and end apart: 29, of which 16 were waited for; matrix products, arithmetic and copies ran while one was open for 6% of the time, Pallas kernels for 26%

profile of v1, /device:TPU:0, one launch (start us, length us, event | category | flops | bytes accessed | tf_op | source)
XLA Modules:
  0.0 391.0 jit_solution(7918803801899638824)
XLA Ops:
  0.6 4.1 %collective-permute-start = (f32[1,256,128]{2,1,0:T(8,128)}, f32[1,256,128]{2,1,0:T(8,128)S(1)}, u32[]{:S(2)}, u32[]{:S(2)}) collective-permute-start(f32[1,256,128]{2,1,0:T(8,128)} %bitcast.30), channel_id=1, source_target_pairs={{0,4},{1,5},{2,6},{3,7},{4,0},{5,1},{6,2},{7,3},{8,12},{9,13},{10,... | collective-permute-start | bytes 393224 | tf_op jit(solution)/shard_map/ppermute | solution.py:276
  4.7 6.5 %collective-permute-done = f32[1,256,128]{2,1,0:T(8,128)S(1)} collective-permute-done((f32[1,256,128]{2,1,0:T(8,128)}, f32[1,256,128]{2,1,0:T(8,128)S(1)}, u32[]{:S(2)}, u32[]{:S(2)}) %collective-permute-start) | collective-permute-done | bytes 131104 | tf_op jit(solution)/shard_map/ppermute | solution.py:276
  13.1 1.3 select_reduce_fusion
  14.4 5.4 %collective-permute-done.1 = f32[2,256,128]{2,1,0:T(8,128)S(1)} collective-permute-done((f32[2,256,128]{2,1,0:T(8,128)S(1)}, f32[2,256,128]{2,1,0:T(8,128)S(1)}, u32[]{:S(2)}, u32[]{:S(2)}) %collective-permute-start.1) | collective-permute-done | bytes 262176 | tf_op jit(solution)/shard_map/ppermute | solution.py:276
  20.7 1.4 collective-permute-start.2
  23.1 5.2 %shard_map.99 = f32[8,96,128]{2,1,0:T(8,128)} custom-call(s32[8]{0:T(128)} %and_select_fusion.3.slots, s32[8]{0:T(128)} %compare_convert_fusion.mine, s32[8]{0:T(128)} %get-tuple-element.6.ranks, f32[32,96,128]{2,1,0:T(8,128)} %bitcast.24), custom_call_target="tpu_custom_call" | custom-call | tf_op jit(solution)/shard_map/pallas_call | solution.py:321
  31.0 1.3 collective-permute-start.3
  34.4 13.6 %collective-permute-done.6 = f32[2,96,128]{2,1,0:T(8,128)S(1)} collective-permute-done((f32[2,96,128]{2,1,0:T(8,128)S(1)}, f32[2,96,128]{2,1,0:T(8,128)S(1)}, u32[]{:S(2)}, u32[]{:S(2)}) %collective-permute-start.6) | collective-permute-done | bytes 98336 | tf_op jit(solution)/shard_map/ppermute | solution.py:337
  48.1 3.2 collective-permute-start.7
  52.8 2.4 constant_dynamic-update-slice_fusion.near
  55.3 1.8 collective-permute-start.8
  57.2 5.5 %collective-permute-done.8 = f32[2,192,128]{2,1,0:T(8,128)S(1)} collective-permute-done((f32[2,192,128]{2,1,0:T(8,128)S(1)}, f32[2,192,128]{2,1,0:T(8,128)S(1)}, u32[]{:S(2)}, u32[]{:S(2)}) %collective-permute-start.8) | collective-permute-done | bytes 196640 | tf_op jit(solution)/shard_map/ppermute | solution.py:276
  62.7 1.6 collective-permute-start.9
  64.3 1.4 broadcast_select_fusion
  65.7 4.3 %all-to-all-start = ((f32[8,4,96,128]{3,2,1,0:T(8,128)}), f32[8,4,96,128]{3,2,1,0:T(8,128)}, u32[]{:S(2)}, u32[]{:S(2)}) async-start(f32[8,4,96,128]{3,2,1,0:T(8,128)} %bitcast.4), calls=%async_computation | async-start | bytes 3145728 | tf_op jit(solution)/shard_map/all_to_all | solution.py:313
  71.5 1.5 collective-permute-start.10
  73.0 1.3 fusion.4
  74.3 1.9 collective-permute-start.19
  79.1 4.7 %collective-permute-done.10 = f32[8,192,128]{2,1,0:T(8,128)} collective-permute-done((f32[8,192,128]{2,1,0:T(8,128)}, f32[8,192,128]{2,1,0:T(8,128)}, u32[]{:S(2)}, u32[]{:S(2)}) %collective-permute-start.10) | collective-permute-done | bytes 786464 | tf_op jit(solution)/shard_map/ppermute | solution.py:276
  83.8 2.1 constant_dynamic-update-slice_fusion.5.refs_3_
  85.9 19.8 %collective-permute-start.11 = (f32[16,192,128]{2,1,0:T(8,128)}, f32[16,192,128]{2,1,0:T(8,128)}, u32[]{:S(2)}, u32[]{:S(2)}) collective-permute-start(f32[16,192,128]{2,1,0:T(8,128)} %constant_dynamic-update-slice_fusion.5.refs_3_), channel_id=1, source_target_pairs={{0,8},{8,0},{16,24},{24,16},{1,9},{9,1},{17,25},{25,17},{2,10},{10... | collective-permute-start | bytes 4718600 | tf_op jit(solution)/shard_map/ppermute | solution.py:278
  105.8 20.4 %shard_map.95.w_in = f32[1024,1024]{1,0:T(8,128)S(1)} custom-call(s32[6]{0:T(128)S(1)} %pad_add_fusion.place.refs_0_, f32[16,256,128]{2,1,0:T(8,128)} %constant_dynamic-update-slice_fusion.near, f32[16,256,128]{2,1,0:T(8,128)} %collective-permute-done.4.far), custom_call_target="tpu_custom_call" | custom-call | flops 4000000000 | bytes 8388608 | tf_op jit(solution)/shard_map/pallas_call | solution.py:111
  126.2 15.3 %shard_map.96.w_in = f32[1024,1024]{1,0:T(8,128)S(1)} custom-call(f32[1024,1024]{1,0:T(8,128)S(1)} %shard_map.95.w_in), custom_call_target="tpu_custom_call" | custom-call | flops 4000000000 | bytes 8388608 | tf_op jit(solution)/shard_map/pallas_call | solution.py:111
  141.5 12.7 %shard_map.97.w_in = f32[1024,1024]{1,0:T(8,128)S(1)} custom-call(f32[1024,1024]{1,0:T(8,128)S(1)} %shard_map.96.w_in), custom_call_target="tpu_custom_call" | custom-call | flops 4000000000 | bytes 8388608 | tf_op jit(solution)/shard_map/pallas_call | solution.py:111
  154.2 9.8 %shard_map.98.refs_1_ = f32[1024,1024]{1,0:T(8,128)S(1)} custom-call(f32[1024,1024]{1,0:T(8,128)S(1)} %shard_map.97.w_in), custom_call_target="tpu_custom_call" | custom-call | flops 4000000000 | bytes 8388608 | tf_op jit(solution)/shard_map/pallas_call | solution.py:111
  164.0 2.0 copy-done.11
  166.0 22.6 %shard_map.100 = (f32[8,384,128]{2,1,0:T(8,128)S(1)}, f32[8,96,384]{2,1,0:T(8,128)S(1)}) custom-call(s32[6]{0:T(128)S(1)} %pad_add_fusion.place.refs_0_, f32[1024,1024]{1,0:T(8,128)} %copy-done.11, f32[8,384,128]{2,1,0:T(8,128)} %bitcast.5.refs_2_, f32[16,192,128]{2,1,0:T(8,128)} %constant_dynamic-update-slice_fusion.5.refs_3_, ...), custom_call_target="tpu_custom_call" | custom-call | flops 6000000000 | bytes 12582912 | tf_op jit(solution)/shard_map/pallas_call | solution.py:390
  190.8 6.7 %all-to-all-start.2 = ((f32[8,96,384]{2,1,0:T(8,128)}), f32[8,96,384]{2,1,0:T(8,128)S(1)}, u32[]{:S(2)}, u32[]{:S(2)}) async-start(f32[8,96,384]{2,1,0:T(8,128)} %copy-done.2), calls=%async_computation.2 | async-start | bytes 2359296 | tf_op jit(solution)/shard_map/all_to_all | solution.py:409
  197.5 2.0 collective-permute-start.20
  199.6 36.3 %collective-permute-done.20.refs_9_ = f32[16,96,128]{2,1,0:T(8,128)S(1)} collective-permute-done((f32[16,96,128]{2,1,0:T(8,128)S(1)}, f32[16,96,128]{2,1,0:T(8,128)S(1)}, u32[]{:S(2)}, u32[]{:S(2)}) %collective-permute-start.20) | collective-permute-done | bytes 786464 | tf_op jit(solution)/shard_map/ppermute | solution.py:358
  236.8 7.8 %collective-permute-start.14 = (f32[16,96,128]{2,1,0:T(8,128)S(1)}, f32[16,96,128]{2,1,0:T(8,128)}, u32[]{:S(2)}, u32[]{:S(2)}) collective-permute-start(f32[16,96,128]{2,1,0:T(8,128)S(1)} %collective-permute-done.13.refs_2_), channel_id=1, source_target_pairs={{0,2},{2,4},{4,6},{6,7},{7,5},{5,3},{3,1},{1,0},{8,10},{10,12},{12... | collective-permute-start | bytes 2359304 | tf_op jit(solution)/shard_map/ppermute | solution.py:357
  245.5 14.9 %collective-permute-done.21.refs_10_ = f32[16,96,128]{2,1,0:T(8,128)} collective-permute-done((f32[16,96,128]{2,1,0:T(8,128)S(1)}, f32[16,96,128]{2,1,0:T(8,128)}, u32[]{:S(2)}, u32[]{:S(2)}) %collective-permute-start.21) | collective-permute-done | bytes 786464 | tf_op jit(solution)/shard_map/ppermute | solution.py:358
  260.4 1.3 collective-permute-done.14.refs_3_
  261.7 1.3 collective-permute-start.15
  263.0 5.2 %all-to-all-start.1 = ((f32[8,384,128]{2,1,0:T(8,128)}), f32[8,384,128]{2,1,0:T(8,128)}, u32[]{:S(2)}, u32[]{:S(2)}) async-start(f32[8,384,128]{2,1,0:T(8,128)} %copy-done.1), calls=%async_computation.1 | async-start | bytes 3145728 | tf_op jit(solution)/shard_map/all_to_all | solution.py:412
  268.3 14.8 %collective-permute-done.22.refs_11_ = f32[16,96,128]{2,1,0:T(8,128)} collective-permute-done((f32[16,96,128]{2,1,0:T(8,128)}, f32[16,96,128]{2,1,0:T(8,128)}, u32[]{:S(2)}, u32[]{:S(2)}) %collective-permute-start.22) | collective-permute-done | bytes 786464 | tf_op jit(solution)/shard_map/ppermute | solution.py:358
  283.1 3.0 collective-permute-start.23
  286.1 2.5 collective-permute-start.16
  288.6 31.9 %collective-permute-done.23.refs_12_ = f32[16,96,128]{2,1,0:T(8,128)S(1)} collective-permute-done((f32[16,96,128]{2,1,0:T(8,128)}, f32[16,96,128]{2,1,0:T(8,128)S(1)}, u32[]{:S(2)}, u32[]{:S(2)}) %collective-permute-start.23) | collective-permute-done | bytes 786464 | tf_op jit(solution)/shard_map/ppermute | solution.py:358
  322.4 9.2 %collective-permute-start.17 = (f32[16,96,128]{2,1,0:T(8,128)S(1)}, f32[16,96,128]{2,1,0:T(8,128)}, u32[]{:S(2)}, u32[]{:S(2)}) collective-permute-start(f32[16,96,128]{2,1,0:T(8,128)S(1)} %collective-permute-done.16.refs_5_), channel_id=1, source_target_pairs={{0,2},{2,4},{4,6},{6,7},{7,5},{5,3},{3,1},{1,0},{8,10},{10,12},{12... | collective-permute-start | bytes 2359304 | tf_op jit(solution)/shard_map/ppermute | solution.py:357
  332.4 13.2 %collective-permute-done.24.refs_13_ = f32[16,96,128]{2,1,0:T(8,128)} collective-permute-done((f32[16,96,128]{2,1,0:T(8,128)S(1)}, f32[16,96,128]{2,1,0:T(8,128)}, u32[]{:S(2)}, u32[]{:S(2)}) %collective-permute-start.24) | collective-permute-done | bytes 786464 | tf_op jit(solution)/shard_map/ppermute | solution.py:358
  345.7 1.9 collective-permute-start.25
  347.6 1.5 collective-permute-done.17.refs_6_
  349.1 1.3 dynamic_slice.26
  355.2 7.0 %collective-permute-done.25.refs_14_ = f32[16,96,128]{2,1,0:T(8,128)} collective-permute-done((f32[16,96,128]{2,1,0:T(8,128)}, f32[16,96,128]{2,1,0:T(8,128)}, u32[]{:S(2)}, u32[]{:S(2)}) %collective-permute-start.25) | collective-permute-done | bytes 786464 | tf_op jit(solution)/shard_map/ppermute | solution.py:358
  362.2 4.6 %collective-permute-done.18.refs_7_ = f32[16,96,128]{2,1,0:T(8,128)} collective-permute-done((f32[16,96,128]{2,1,0:T(8,128)}, f32[16,96,128]{2,1,0:T(8,128)}, u32[]{:S(2)}, u32[]{:S(2)}) %collective-permute-start.18) | collective-permute-done | bytes 786464 | tf_op jit(solution)/shard_map/ppermute | solution.py:357
  371.3 16.6 %shard_map.101 = f32[32,1,96,1024]{3,2,1,0:T(8,128)} custom-call(s32[15]{0:T(128)S(1)} %add_multiply_fusion.offs, s32[32]{0:T(128)S(1)} %dynamic_slice.21.ranks, s32[32]{0:T(128)S(1)} %dynamic_slice.27.tiles, s32[1]{0:T(128)} %bitcast.1.col, f32[8,96,384]{2,1,0:T(8,128)S(1)} %all-to-all-done.2.core, f32[32,96,128]{2,1,0:T(8,128)S(1)} %bitcast.22, ...), custom_call_target="tpu_custom_call" | custom-call | tf_op jit(solution)/shard_map/pallas_call | solution.py:424
  387.9 2.7 copy.19
  (92 shorter events, 31.0 us)
Async XLA Ops:
  0.6 10.6 %collective-permute-start = (f32[1,256,128]{2,1,0:T(8,128)}, f32[1,256,128]{2,1,0:T(8,128)S(1)}, u32[]{:S(2)}, u32[]{:S(2)}) collective-permute-start(f32[1,256,128]{2,1,0:T(8,128)} %bitcast.30), channel_id=1, source_target_pairs={{0,4},{1,5},{2,6},{3,7},{4,0},{5,1},{6,2},{7,3},{8,12},{9,13},{10,... | collective-permute-start | bytes 393224 | tf_op jit(solution)/shard_map/ppermute | solution.py:276
  12.2 7.6 %collective-permute-start.1 = (f32[2,256,128]{2,1,0:T(8,128)S(1)}, f32[2,256,128]{2,1,0:T(8,128)S(1)}, u32[]{:S(2)}, u32[]{:S(2)}) collective-permute-start(f32[2,256,128]{2,1,0:T(8,128)S(1)} %pad_maximum_fusion.4), channel_id=1, source_target_pairs={{0,2},{1,3},{2,0},{3,1},{4,6},{5,7},{6,4},{7,5},{8,10},{9,11},{10,... | collective-permute-start | bytes 786440 | tf_op jit(solution)/shard_map/ppermute | solution.py:276
  14.4 15.6 %copy-start.14 = (f32[256,128]{1,0:T(8,128)S(1)}, f32[256,128]{1,0:T(8,128)}, u32[]{:S(2)}) copy-start(f32[256,128]{1,0:T(8,128)} %param.8) | copy-start | bytes 393220
  20.7 9.2 %collective-permute-start.2 = (f32[4,256,128]{2,1,0:T(8,128)S(1)}, f32[4,256,128]{2,1,0:T(8,128)S(1)}, u32[]{:S(2)}, u32[]{:S(2)}) collective-permute-start(f32[4,256,128]{2,1,0:T(8,128)S(1)} %pad_maximum_fusion.2), channel_id=1, source_target_pairs={{0,1},{1,0},{2,3},{3,2},{4,5},{5,4},{6,7},{7,6},{8,24},{9,25},{10,... | collective-permute-start | bytes 1572872 | tf_op jit(solution)/shard_map/ppermute | solution.py:276
  28.3 4.6 %copy-start.15 = (f32[8,96,128]{2,1,0:T(8,128)S(1)}, f32[8,96,128]{2,1,0:T(8,128)}, u32[]{:S(2)}) copy-start(f32[8,96,128]{2,1,0:T(8,128)} %shard_map.99) | copy-start | bytes 1179652
  29.4 3.6 collective-permute-start.5
  31.0 21.8 %collective-permute-start.3 = (f32[8,256,128]{2,1,0:T(8,128)}, f32[8,256,128]{2,1,0:T(8,128)}, u32[]{:S(2)}, u32[]{:S(2)}) collective-permute-start(f32[8,256,128]{2,1,0:T(8,128)} %pad_maximum_fusion), channel_id=1, source_target_pairs={{0,16},{1,17},{2,18},{3,19},{4,20},{5,21},{6,22},{7,23},{8,9},{9,8... | collective-permute-start | bytes 3145736 | tf_op jit(solution)/shard_map/ppermute | solution.py:276
  33.0 15.1 %collective-permute-start.6 = (f32[2,96,128]{2,1,0:T(8,128)S(1)}, f32[2,96,128]{2,1,0:T(8,128)S(1)}, u32[]{:S(2)}, u32[]{:S(2)}) collective-permute-start(f32[2,96,128]{2,1,0:T(8,128)S(1)} %constant_dynamic-slice_fusion), channel_id=1, source_target_pairs={{0,16},{8,24},{16,0},{24,8},{1,17},{9,25},{17,1},{25,9},{2,18},{10... | collective-permute-start | bytes 294920 | tf_op jit(solution)/shard_map/ppermute | solution.py:337
  48.1 7.2 %collective-permute-start.7 = (f32[1,192,128]{2,1,0:T(8,128)S(1)}, f32[1,192,128]{2,1,0:T(8,128)S(1)}, u32[]{:S(2)}, u32[]{:S(2)}) collective-permute-start(f32[1,192,128]{2,1,0:T(8,128)S(1)} %bitcast.25), channel_id=1, source_target_pairs={{0,4},{1,5},{2,6},{3,7},{4,0},{5,1},{6,2},{7,3},{8,12},{9,13},{10,... | collective-permute-start | bytes 294920 | tf_op jit(solution)/shard_map/ppermute | solution.py:276
  52.0 3.2 copy-start.16
  52.8 11.5 %copy-start.13 = (f32[32,128,96]{1,2,0:T(8,128)S(1)}, f32[32,128,96]{1,2,0:T(8,128)}, u32[]{:S(2)}) copy-start(f32[32,128,96]{1,2,0:T(8,128)} %param.10) | copy-start | bytes 4718596
  55.2 50.6 %collective-permute-start.4 = (f32[16,256,128]{2,1,0:T(8,128)}, f32[16,256,128]{2,1,0:T(8,128)}, u32[]{:S(2)}, u32[]{:S(2)}) collective-permute-start(f32[16,256,128]{2,1,0:T(8,128)} %constant_dynamic-update-slice_fusion.near), channel_id=1, source_target_pairs={{0,8},{8,0},{16,24},{24,16},{1,9},{9,1},{17,25},{25,17},{2,10},{10... | collective-permute-start | bytes 6291464 | tf_op jit(solution)/shard_map/ppermute | solution.py:278
  55.3 7.4 %collective-permute-start.8 = (f32[2,192,128]{2,1,0:T(8,128)S(1)}, f32[2,192,128]{2,1,0:T(8,128)S(1)}, u32[]{:S(2)}, u32[]{:S(2)}) collective-permute-start(f32[2,192,128]{2,1,0:T(8,128)S(1)} %pad_maximum_fusion.5), channel_id=1, source_target_pairs={{0,2},{1,3},{2,0},{3,1},{4,6},{5,7},{6,4},{7,5},{8,10},{9,11},{10,... | collective-permute-start | bytes 589832 | tf_op jit(solution)/shard_map/ppermute | solution.py:276
  62.7 7.8 %collective-permute-start.9 = (f32[4,192,128]{2,1,0:T(8,128)S(1)}, f32[4,192,128]{2,1,0:T(8,128)S(1)}, u32[]{:S(2)}, u32[]{:S(2)}) collective-permute-start(f32[4,192,128]{2,1,0:T(8,128)S(1)} %pad_maximum_fusion.3), channel_id=1, source_target_pairs={{0,1},{1,0},{2,3},{3,2},{4,5},{5,4},{6,7},{7,6},{8,24},{9,25},{10,... | collective-permute-start | bytes 1179656 | tf_op jit(solution)/shard_map/ppermute | solution.py:276
  65.7 100.3 %all-to-all-start = ((f32[8,4,96,128]{3,2,1,0:T(8,128)}), f32[8,4,96,128]{3,2,1,0:T(8,128)}, u32[]{:S(2)}, u32[]{:S(2)}) async-start(f32[8,4,96,128]{3,2,1,0:T(8,128)} %bitcast.4), calls=%async_computation | async-start | bytes 3145728 | tf_op jit(solution)/shard_map/all_to_all | solution.py:313
  70.0 3.0 copy-start
  71.5 12.3 %collective-permute-start.10 = (f32[8,192,128]{2,1,0:T(8,128)}, f32[8,192,128]{2,1,0:T(8,128)}, u32[]{:S(2)}, u32[]{:S(2)}) collective-permute-start(f32[8,192,128]{2,1,0:T(8,128)} %pad_maximum_fusion.1), channel_id=1, source_target_pairs={{0,16},{1,17},{2,18},{3,19},{4,20},{5,21},{6,22},{7,23},{8,9},{9,8... | collective-permute-start | bytes 2359304 | tf_op jit(solution)/shard_map/ppermute | solution.py:276
  74.3 123.2 %collective-permute-start.19 = (f32[16,96,128]{2,1,0:T(8,128)}, f32[16,96,128]{2,1,0:T(8,128)S(1)}, u32[]{:S(2)}, u32[]{:S(2)}) collective-permute-start(f32[16,96,128]{2,1,0:T(8,128)} %get-tuple-element.8), channel_id=1, source_target_pairs={{2,0},{4,2},{6,4},{7,6},{5,7},{3,5},{1,3},{0,1},{10,8},{12,10},{14... | collective-permute-start | bytes 2359304 | tf_op jit(solution)/shard_map/ppermute | solution.py:358
  76.3 123.3 %collective-permute-start.12 = (f32[16,96,128]{2,1,0:T(8,128)}, f32[16,96,128]{2,1,0:T(8,128)}, u32[]{:S(2)}, u32[]{:S(2)}) collective-permute-start(f32[16,96,128]{2,1,0:T(8,128)} %get-tuple-element.9), channel_id=1, source_target_pairs={{0,2},{2,4},{4,6},{6,7},{7,5},{5,3},{3,1},{1,0},{8,10},{10,12},{12... | collective-permute-start | bytes 2359304 | tf_op jit(solution)/shard_map/ppermute | solution.py:357
  76.4 29.4 %copy-start.18 = (s32[4]{0:T(128)S(1)}, s32[4]{0:T(128)}, u32[]{:S(2)}) copy-start(s32[4]{0:T(128)} %constant.106.clone) | copy-start | bytes 52
  85.9 80.1 %collective-permute-start.11 = (f32[16,192,128]{2,1,0:T(8,128)}, f32[16,192,128]{2,1,0:T(8,128)}, u32[]{:S(2)}, u32[]{:S(2)}) collective-permute-start(f32[16,192,128]{2,1,0:T(8,128)} %constant_dynamic-update-slice_fusion.5.refs_3_), channel_id=1, source_target_pairs={{0,8},{8,0},{16,24},{24,16},{1,9},{9,1},{17,25},{25,17},{2,10},{10... | collective-permute-start | bytes 4718600 | tf_op jit(solution)/shard_map/ppermute | solution.py:278
  164.0 2.0 copy-start.11
  188.6 1.1 copy-start.1
  189.8 1.0 copy-start.2
  190.8 72.2 %all-to-all-start.2 = ((f32[8,96,384]{2,1,0:T(8,128)}), f32[8,96,384]{2,1,0:T(8,128)S(1)}, u32[]{:S(2)}, u32[]{:S(2)}) async-start(f32[8,96,384]{2,1,0:T(8,128)} %copy-done.2), calls=%async_computation.2 | async-start | bytes 2359296 | tf_op jit(solution)/shard_map/all_to_all | solution.py:409
  197.5 38.4 %collective-permute-start.20 = (f32[16,96,128]{2,1,0:T(8,128)S(1)}, f32[16,96,128]{2,1,0:T(8,128)S(1)}, u32[]{:S(2)}, u32[]{:S(2)}) collective-permute-start(f32[16,96,128]{2,1,0:T(8,128)S(1)} %collective-permute-done.19.refs_8_), channel_id=1, source_target_pairs={{2,0},{4,2},{6,4},{7,6},{5,7},{3,5},{1,3},{0,1},{10,8},{12,10},{14... | collective-permute-start | bytes 2359304 | tf_op jit(solution)/shard_map/ppermute | solution.py:358
  199.5 37.2 %collective-permute-start.13 = (f32[16,96,128]{2,1,0:T(8,128)}, f32[16,96,128]{2,1,0:T(8,128)S(1)}, u32[]{:S(2)}, u32[]{:S(2)}) collective-permute-start(f32[16,96,128]{2,1,0:T(8,128)} %collective-permute-done.12.refs_1_), channel_id=1, source_target_pairs={{0,2},{2,4},{4,6},{6,7},{7,5},{5,3},{3,1},{1,0},{8,10},{10,12},{12... | collective-permute-start | bytes 2359304 | tf_op jit(solution)/shard_map/ppermute | solution.py:357
  235.9 24.5 %collective-permute-start.21 = (f32[16,96,128]{2,1,0:T(8,128)S(1)}, f32[16,96,128]{2,1,0:T(8,128)}, u32[]{:S(2)}, u32[]{:S(2)}) collective-permute-start(f32[16,96,128]{2,1,0:T(8,128)S(1)} %collective-permute-done.20.refs_9_), channel_id=1, source_target_pairs={{2,0},{4,2},{6,4},{7,6},{5,7},{3,5},{1,3},{0,1},{10,8},{12,10},{14... | collective-permute-start | bytes 2359304 | tf_op jit(solution)/shard_map/ppermute | solution.py:358
  235.9 0.9 copy-start.3
  236.8 25.0 %collective-permute-start.14 = (f32[16,96,128]{2,1,0:T(8,128)S(1)}, f32[16,96,128]{2,1,0:T(8,128)}, u32[]{:S(2)}, u32[]{:S(2)}) collective-permute-start(f32[16,96,128]{2,1,0:T(8,128)S(1)} %collective-permute-done.13.refs_2_), channel_id=1, source_target_pairs={{0,2},{2,4},{4,6},{6,7},{7,5},{5,3},{3,1},{1,0},{8,10},{10,12},{12... | collective-permute-start | bytes 2359304 | tf_op jit(solution)/shard_map/ppermute | solution.py:357
  244.6 0.9 copy-start.5
  260.4 22.7 %collective-permute-start.22 = (f32[16,96,128]{2,1,0:T(8,128)}, f32[16,96,128]{2,1,0:T(8,128)}, u32[]{:S(2)}, u32[]{:S(2)}) collective-permute-start(f32[16,96,128]{2,1,0:T(8,128)} %collective-permute-done.21.refs_10_), channel_id=1, source_target_pairs={{2,0},{4,2},{6,4},{7,6},{5,7},{3,5},{1,3},{0,1},{10,8},{12,10},{14... | collective-permute-start | bytes 2359304 | tf_op jit(solution)/shard_map/ppermute | solution.py:358
  261.7 24.3 %collective-permute-start.15 = (f32[16,96,128]{2,1,0:T(8,128)}, f32[16,96,128]{2,1,0:T(8,128)}, u32[]{:S(2)}, u32[]{:S(2)}) collective-permute-start(f32[16,96,128]{2,1,0:T(8,128)} %collective-permute-done.14.refs_3_), channel_id=1, source_target_pairs={{0,2},{2,4},{4,6},{6,7},{7,5},{5,3},{3,1},{1,0},{8,10},{10,12},{12... | collective-permute-start | bytes 2359304 | tf_op jit(solution)/shard_map/ppermute | solution.py:357
  263.0 86.0 %copy-start.17 = (s32[128]{0:T(128)S(1)}, s32[128]{0:T(128)}, u32[]{:S(2)}) copy-start(s32[128]{0:T(128)} %param.12) | copy-start | bytes 1540
  263.0 88.5 %copy-start.12 = (s32[8]{0:T(128)S(1)}, s32[8]{0:T(128)}, u32[]{:S(2)}) copy-start(s32[8]{0:T(128)} %constant.108.clone) | copy-start | bytes 100
  263.0 124.9 %all-to-all-start.1 = ((f32[8,384,128]{2,1,0:T(8,128)}), f32[8,384,128]{2,1,0:T(8,128)}, u32[]{:S(2)}, u32[]{:S(2)}) async-start(f32[8,384,128]{2,1,0:T(8,128)} %copy-done.1), calls=%async_computation.1 | async-start | bytes 3145728 | tf_op jit(solution)/shard_map/all_to_all | solution.py:412
  283.1 37.3 %collective-permute-start.23 = (f32[16,96,128]{2,1,0:T(8,128)}, f32[16,96,128]{2,1,0:T(8,128)S(1)}, u32[]{:S(2)}, u32[]{:S(2)}) collective-permute-start(f32[16,96,128]{2,1,0:T(8,128)} %collective-permute-done.22.refs_11_), channel_id=1, source_target_pairs={{2,0},{4,2},{6,4},{7,6},{5,7},{3,5},{1,3},{0,1},{10,8},{12,10},{14... | collective-permute-start | bytes 2359304 | tf_op jit(solution)/shard_map/ppermute | solution.py:358
  286.1 36.3 %collective-permute-start.16 = (f32[16,96,128]{2,1,0:T(8,128)}, f32[16,96,128]{2,1,0:T(8,128)S(1)}, u32[]{:S(2)}, u32[]{:S(2)}) collective-permute-start(f32[16,96,128]{2,1,0:T(8,128)} %collective-permute-done.15.refs_4_), channel_id=1, source_target_pairs={{0,2},{2,4},{4,6},{6,7},{7,5},{5,3},{3,1},{1,0},{8,10},{10,12},{12... | collective-permute-start | bytes 2359304 | tf_op jit(solution)/shard_map/ppermute | solution.py:357
  320.4 25.3 %collective-permute-start.24 = (f32[16,96,128]{2,1,0:T(8,128)S(1)}, f32[16,96,128]{2,1,0:T(8,128)}, u32[]{:S(2)}, u32[]{:S(2)}) collective-permute-start(f32[16,96,128]{2,1,0:T(8,128)S(1)} %collective-permute-done.23.refs_12_), channel_id=1, source_target_pairs={{2,0},{4,2},{6,4},{7,6},{5,7},{3,5},{1,3},{0,1},{10,8},{12,10},{14... | collective-permute-start | bytes 2359304 | tf_op jit(solution)/shard_map/ppermute | solution.py:358
  321.5 0.9 copy-start.7
  322.4 26.6 %collective-permute-start.17 = (f32[16,96,128]{2,1,0:T(8,128)S(1)}, f32[16,96,128]{2,1,0:T(8,128)}, u32[]{:S(2)}, u32[]{:S(2)}) collective-permute-start(f32[16,96,128]{2,1,0:T(8,128)S(1)} %collective-permute-done.16.refs_5_), channel_id=1, source_target_pairs={{0,2},{2,4},{4,6},{6,7},{7,5},{5,3},{3,1},{1,0},{8,10},{10,12},{12... | collective-permute-start | bytes 2359304 | tf_op jit(solution)/shard_map/ppermute | solution.py:357
  331.6 0.9 copy-start.9
  345.7 16.5 %collective-permute-start.25 = (f32[16,96,128]{2,1,0:T(8,128)}, f32[16,96,128]{2,1,0:T(8,128)}, u32[]{:S(2)}, u32[]{:S(2)}) collective-permute-start(f32[16,96,128]{2,1,0:T(8,128)} %collective-permute-done.24.refs_13_), channel_id=1, source_target_pairs={{2,0},{4,2},{6,4},{7,6},{5,7},{3,5},{1,3},{0,1},{10,8},{12,10},{14... | collective-permute-start | bytes 2359304 | tf_op jit(solution)/shard_map/ppermute | solution.py:358
  349.0 17.7 %collective-permute-start.18 = (f32[16,96,128]{2,1,0:T(8,128)}, f32[16,96,128]{2,1,0:T(8,128)}, u32[]{:S(2)}, u32[]{:S(2)}) collective-permute-start(f32[16,96,128]{2,1,0:T(8,128)} %collective-permute-done.17.refs_6_), channel_id=1, source_target_pairs={{0,2},{2,4},{4,6},{6,7},{7,5},{5,3},{3,1},{1,0},{8,10},{10,12},{12... | collective-permute-start | bytes 2359304 | tf_op jit(solution)/shard_map/ppermute | solution.py:357
  366.8 1.1 copy-start.4
  367.9 1.1 copy-start.6
  369.0 1.1 copy-start.8
  370.2 1.1 copy-start.10
